TPU v7x, 32 devices: a whole 2x2x4 slice. The times are simulated.
32 devices in a mesh: row: 4 (over y, core), col: 8 (over z, x).
Axes of the slice: x: 2, y: 2, z: 4, core: 2. Of those that a mesh axis runs over, the one named last changes fastest.
Arguments:
- fisher: float32 [16384, 16384], P('row', 'col'), may hold values from -6 to 6
- slab: float32 [256, 16384], P(('row', 'col')), may hold values from -6 to 6
Outputs:
- fisher_out: float32 [16384, 16384], P('row', 'col')
All inputs are finite; a program needn't handle non-finite values.
Results may differ from a plain program's by a relative error of at most 0.00005.
Values sent between devices are 32-bit elements; how exact they have to be, the bound alone decides.
A program may use at most 128 MiB of HBM per device.

v0:
```python
import jax
import jax.numpy as jnp
from jax import lax
from jax.sharding import PartitionSpec as P


def transposed_product(left, right):
    return lax.dot_general(
        left,
        right,
        (((0, 1, 2), (0, 1, 2)), ((), ())),
        precision=lax.Precision.HIGHEST,
        preferred_element_type=jnp.float32,
    )


def row_panel(slab, n_row, t_row):
    rows = slab.shape[0]
    pieces = lax.all_to_all(
        slab.reshape(rows, n_row, t_row), "row", split_axis=1, concat_axis=1, tiled=True
    )
    return lax.all_gather(pieces.reshape(rows, n_row, 1, t_row), "col", axis=2, tiled=True)


def col_pieces(slab, n_col, t_col):
    rows = slab.shape[0]
    pieces = lax.all_to_all(
        slab.reshape(rows, n_col, t_col), "col", split_axis=1, concat_axis=1, tiled=True
    )
    return pieces.reshape(rows, 1, n_col, t_col)


def direct_product(slab, n_row, n_col, t_row, t_col):
    left = row_panel(slab, n_row, t_row)
    local_right = col_pieces(slab, n_col, t_col)
    return transposed_product(left, lax.all_gather(local_right, "row", axis=1, tiled=True))


def body(fisher, slab):
    n_row = lax.axis_size("row")
    n_col = lax.axis_size("col")
    order = slab.shape[1]
    t_row = order // n_row
    t_col = order // n_col
    examples = slab.shape[0] * n_row * n_col
    product = direct_product(slab, n_row, n_col, t_row, t_col)
    return fisher + product / examples


def solution(mesh):
    return jax.shard_map(
        body,
        mesh=mesh,
        in_specs=(P("row", "col"), P(("row", "col"), None)),
        out_specs=P("row", "col"),
        check_vma=False,
    )
```

profile of v0, /device:TPU:0, one launch (start us, length us, event | category | flops | bytes accessed | tf_op | source)
XLA Modules:
  0.0 170.3 jit_solution(4026029849138574522)
XLA Ops:
  6.5 0.0 all-gather.5.cloned.1.call-start
  6.5 13.7 %all_to_all.10 = f32[8,4,4096]{2,0,1:T(8,128)} all-to-all(f32[8,4,4096]{2,0,1:T(8,128)} %bitcast.27), channel_id=1, replica_groups=mesh['row'=4,'col'=8] {'row'}, dimensions={1} | all-to-all | bytes 1048576 | tf_op jit(solution)/shard_map/all_to_all | solution.py:19
  20.2 0.0 all-gather.5.cloned.1.call-update
  20.3 0.0 all-gather.7.cloned.1.call-start
  20.3 32.0 %all_to_all.11 = f32[8,8,2048]{2,0,1:T(8,128)} all-to-all(f32[8,8,2048]{2,0,1:T(8,128)} %bitcast.28), channel_id=1, replica_groups=mesh['row'=4,'col'=8] {'col'}, dimensions={1} | all-to-all | bytes 1048576 | tf_op jit(solution)/shard_map/all_to_all | solution.py:27
  52.3 0.0 all-gather.7.cloned.1.call-update
  52.3 49.2 %all-gather.5.cloned.1.call-done = f32[8,4,32768]{2,0,1:T(8,128)} async-done(((f32[8,4,4096]{2,0,1:T(8,128)}), f32[8,4,32768]{2,0,1:T(8,128)}) %all-gather.5.cloned.1.call-update) | async-done | bytes 4194320 | tf_op jit(solution)/shard_map/all_gather | solution.py:22
  101.5 6.6 %fusion.7 = f32[8,4,8,4096]{3,2,1,0:T(8,128)} fusion(f32[4,8,8,4096]{3,1,2,0:T(8,128)} %bitcast.26), kind=kLoop, calls=%fused_computation.3.clone.1 | loop fusion | bytes 8388608 | tf_op jit(solution)/shard_map/dot_general | solution.py:8
  108.1 15.9 %all-gather.7.cloned.1.call-done = f32[8,32,2048]{2,0,1:T(8,128)} async-done(((f32[8,8,2048]{2,0,1:T(8,128)}), f32[8,32,2048]{2,0,1:T(8,128)}) %all-gather.7.cloned.1.call-update) | async-done | bytes 2097168 | tf_op jit(solution)/shard_map/all_gather | solution.py:36
  123.9 39.5 %fusion = f32[4096,2048]{1,0:T(8,128)} fusion(f32[4096,2048]{1,0:T(8,128)} %param.2, f32[8,32,2048]{2,0,1:T(8,128)} %all-gather.7.cloned.1.call-done, f32[8,4,8,4096]{3,2,1,0:T(8,128)} %fusion.7), kind=kOutput, calls=%fused_computation.1 | convolution fusion | flops 25786580992 | bytes 73400320 | tf_op jit(solution)/shard_map/dot_general | solution.py:8
Async XLA Ops:
  6.5 94.9 %all-gather.5.cloned.1.call-start = ((), (), s32[]{:S(2)}) async-start(), calls=%async_computation.2 | async-start | bytes 4718592 | tf_op jit(solution)/shard_map/all_gather | solution.py:22
  20.3 103.7 %all-gather.7.cloned.1.call-start = ((), (), s32[]{:S(2)}) async-start(), calls=%async_computation.3 | async-start | bytes 2621440 | tf_op jit(solution)/shard_map/all_gather | solution.py:36
Sparse Core Ops, SparseCore 0:
  20.4 81.0 all-gather.4
  103.0 20.8 all-gather.6
where the time goes:
time: 171 us; the launch traced here: 170 us
  waiting for transfers between devices  65.1 us (38%)
  blocking collectives  45.6 us (27%)
  matrix products  39.5 us (23%)
  between operations  13.4 us (8%)
  local copies, waits for them, and re-layouts  6.59 us (4%)
    all_gather x1, waiting for transfers between devices, row_panel(): lax.all_gather(pieces.reshape(rows, n_row, 1, t_row), 'col', axis=2, tile...  49.2 us
    dot_general x1, matrix products, transposed_product(): lax.dot_general(left, right, (((0, 1, 2), (0, 1, 2)), ((), ())), precisio...  39.5 us
    all_to_all x1, blocking collectives, col_pieces(): lax.all_to_all(slab.reshape(rows, n_col, t_col), 'col', split_axis=1, con...  32 us
    all_gather x1, waiting for transfers between devices, direct_product(): lax.all_gather(local_right, 'row', axis=1, tiled=True)  15.9 us
    all_to_all x1, blocking collectives, row_panel(): lax.all_to_all(slab.reshape(rows, n_row, t_row), 'row', split_axis=1, con...  13.7 us
    dot_general x1, local copies, waits for them, and re-layouts, transposed_product(): lax.dot_general(left, right, (((0, 1, 2), (0, 1, 2)), ((), ())), precisio...  6.59 us
  transfers between devices with their start and end apart: 2, of which 2 were waited for; matrix products, arithmetic and copies ran while one was open for 4% of the time, Pallas kernels for 0%

commit v1 on v0

v1 whole, which is shorter than its diff:
```python
import functools

import jax
import jax.numpy as jnp
from jax import lax
from jax.experimental import pallas as pl
from jax.experimental.pallas import tpu as pltpu
from jax.sharding import PartitionSpec as P

MESH = pl.DeviceIdType.MESH


def gather_kernel(n_row, n_col, slab_ref, row_ref, col_ref, send_a, recv_a, send_g, recv_g, send_c, recv_c, local):
    t_row, t_col = row_ref.shape[3], col_ref.shape[3]
    r, c = lax.axis_index("row"), lax.axis_index("col")
    n_x = 2
    n_z = n_col // n_x
    z, x = c // n_x, c % n_x
    owner = c * t_col // t_row
    offset = pl.multiple_of(c * t_col - owner * t_row, t_col)
    sibling = r + 1 - 2 * (r % 2)
    leader = r % 2 == owner % 2
    is_owner = r == owner

    barrier = pltpu.get_barrier_semaphore()

    def greet_row(i, _):
        pl.semaphore_signal(barrier, inc=1, device_id=(lax.rem(r + i, n_row), c), device_id_type=MESH)
        return 0

    lax.fori_loop(1, n_row, greet_row, 0)
    has_up, has_down = z < n_z - 1, z > 0
    across = z * n_x + 1 - x
    pl.semaphore_signal(barrier, inc=1, device_id=(r, across), device_id_type=MESH)

    @pl.when(has_up)
    def _():
        pl.semaphore_signal(barrier, inc=1, device_id=(r, c + n_x), device_id_type=MESH)

    @pl.when(has_down)
    def _():
        pl.semaphore_signal(barrier, inc=1, device_id=(r, c - n_x), device_id_type=MESH)

    pl.semaphore_wait(barrier, n_row + has_up.astype(jnp.int32) + has_down.astype(jnp.int32))

    def tile(q):
        return slab_ref.at[:, pl.ds(pl.multiple_of(q * t_row, t_row), t_row)]

    def exchange(i):
        q = lax.rem(r + i, n_row)
        return pltpu.make_async_remote_copy(
            src_ref=tile(q), dst_ref=row_ref.at[c, r], send_sem=send_a.at[q], recv_sem=recv_a.at[r],
            device_id=(q, c), device_id_type=MESH)

    def arrival(q):
        return pltpu.make_async_remote_copy(
            src_ref=tile(q), dst_ref=row_ref.at[c, q], send_sem=send_a.at[q], recv_sem=recv_a.at[q],
            device_id=(q, c), device_id_type=MESH)

    def move(way, k, q):
        to = (c + n_x, c - n_x, across)[way]
        return pltpu.make_async_remote_copy(
            src_ref=row_ref.at[k, q], dst_ref=row_ref.at[k, q], send_sem=send_g.at[way, k, q], recv_sem=recv_g.at[k, q],
            device_id=(r, to), device_id_type=MESH)

    def spread(k, p):
        return pltpu.make_async_remote_copy(
            src_ref=row_ref.at[k, :, :, pl.ds(offset, t_col)], dst_ref=col_ref.at[k], send_sem=send_c.at[k, p],
            recv_sem=recv_c.at[k], device_id=(2 * p + owner % 2, c), device_id_type=MESH)

    def to_sibling(k):
        return pltpu.make_async_remote_copy(
            src_ref=col_ref.at[k], dst_ref=col_ref.at[k], send_sem=send_c.at[k, r // 2],
            recv_sem=recv_c.at[k], device_id=(sibling, c), device_id_type=MESH)

    def owner_to_sibling(k):
        return pltpu.make_async_remote_copy(
            src_ref=row_ref.at[k, :, :, pl.ds(offset, t_col)], dst_ref=col_ref.at[k], send_sem=send_c.at[k, r // 2],
            recv_sem=recv_c.at[k], device_id=(sibling, c), device_id_type=MESH)

    def own_columns(k):
        return pltpu.make_async_copy(row_ref.at[k, :, :, pl.ds(offset, t_col)], col_ref.at[k], recv_c.at[k])

    def for_pairs(what, k):
        def one(p, _):
            @pl.when(p != r // 2)
            def _():
                what(spread(k, p))
            return 0

        lax.fori_loop(0, n_row // 2, one, 0)

    def spread_block(k):
        @pl.when(is_owner)
        def _():
            for_pairs(lambda copy: copy.start(), k)
            owner_to_sibling(k).start()
            own_columns(k).start()

    def pass_on(k):
        @pl.when(leader & ~is_owner)
        def _():
            to_sibling(k).wait_recv()
            to_sibling(k).start()

    def exchange_one(i, _):
        exchange(i).start()
        return 0

    mine = pltpu.make_async_copy(tile(r), row_ref.at[c, r], local)
    mine.start()
    lax.fori_loop(1, n_row, exchange_one, 0)
    mine.wait()

    def send_own(i, _):
        q = lax.rem(r + n_row - i, n_row)

        @pl.when(i > 0)
        def _():
            arrival(q).wait_recv()

        @pl.when(has_up)
        def _():
            move(0, c, q).start()

        @pl.when(has_down)
        def _():
            move(1, c, q).start()

        move(2, c, q).start()
        return 0

    lax.fori_loop(0, n_row, send_own, 0)
    spread_block(c)

    def received(k):
        def one(i, _):
            move(2, k, lax.rem(r + n_row - i, n_row)).wait_recv()
            return 0

        lax.fori_loop(0, n_row, one, 0)

    def crossed(s):
        for k, there in ((across - s * n_x, z >= s), (across + s * n_x, z + s < n_z)):
            if s == 0 and k is not None:
                there = True

            def both(k=k):
                received(k)
                spread_block(k)

            if s == 0:
                both()
                return
            pl.when(there)(both)

    def passed(s):
        if s == 0:
            pass_on(c)
            pass_on(across)
            return
        for k, there in ((c - s * n_x, z >= s), (c + s * n_x, z + s < n_z)):
            def both(k=k):
                pass_on(k)
                pass_on(k + 1 - 2 * x)

            pl.when(there)(both)

    for s in range(1, n_z):
        def step(i, _, s=s):
            q = lax.rem(r + n_row - i, n_row)

            @pl.when(z >= s)
            def _():
                k = c - s * n_x
                move(0, k, q).wait_recv()

                @pl.when(has_up)
                def _():
                    move(0, k, q).start()

                move(2, k, q).start()

            @pl.when(z + s < n_z)
            def _():
                k = c + s * n_x
                move(1, k, q).wait_recv()

                @pl.when(has_down)
                def _():
                    move(1, k, q).start()

                move(2, k, q).start()
            return 0

        lax.fori_loop(0, n_row, step, 0)
        for k, there in ((c - s * n_x, z >= s), (c + s * n_x, z + s < n_z)):
            pl.when(there)(functools.partial(spread_block, k))
        if s >= 2:
            crossed(s - 2)
            passed(s - 2)
    for s in range(max(n_z - 2, 0), n_z):
        crossed(s)
    for s in range(max(n_z - 2, 0), n_z):
        passed(s)

    def sent_own(i, _):
        exchange(i).wait_send()
        return 0

    lax.fori_loop(1, n_row, sent_own, 0)

    def finish(k, _):
        same = k % n_x == x

        def one(q, _):
            @pl.when(same)
            def _():
                move(2, k, q).wait_send()

            @pl.when(same & has_up & (k <= c))
            def _():
                move(0, k, q).wait_send()

            @pl.when(same & has_down & (k >= c))
            def _():
                move(1, k, q).wait_send()
            return 0

        lax.fori_loop(0, n_row, one, 0)

        @pl.when(is_owner)
        def _():
            for_pairs(lambda copy: copy.wait_send(), k)
            owner_to_sibling(k).wait_send()
            own_columns(k).wait()

        @pl.when(leader & ~is_owner)
        def _():
            to_sibling(k).wait_send()

        @pl.when(~leader)
        def _():
            to_sibling(k).wait_recv()
        return 0

    lax.fori_loop(0, n_col, finish, 0)


def gather(slab, n_row, n_col, t_row, t_col):
    rows = slab.shape[0]
    dma = pltpu.SemaphoreType.DMA
    return pl.pallas_call(
        functools.partial(gather_kernel, n_row, n_col),
        out_shape=(
            jax.ShapeDtypeStruct((n_col, n_row, rows, t_row), jnp.float32),
            jax.ShapeDtypeStruct((n_col, n_row, rows, t_col), jnp.float32),
        ),
        in_specs=[pl.BlockSpec(memory_space=pl.ANY)],
        out_specs=(pl.BlockSpec(memory_space=pl.ANY),) * 2,
        scratch_shapes=[
            dma((n_row,)), dma((n_row,)), dma((3, n_col, n_row)), dma((n_col, n_row)),
            dma((n_col, n_row // 2)), dma((n_col,)), dma(()),
        ],
        compiler_params=pltpu.CompilerParams(collective_id=0, has_side_effects=True),
        name="gather_panels",
    )(slab)


def split(values):
    high = values.astype(jnp.bfloat16)
    low = (values - high.astype(jnp.float32)).astype(jnp.bfloat16)
    return high, low


def add_kernel(examples, fisher_ref, left_ref, right_ref, out_ref, split_right):
    depth = right_ref.shape[0]

    @pl.when(pl.program_id(0) == 0)
    def _():
        high, low = split(right_ref[...])
        split_right[0:depth] = high
        split_right[depth : 2 * depth] = low
        split_right[2 * depth :] = high

    high, low = split(left_ref[...])
    left = jnp.concatenate([high, high, low], axis=0)
    product = lax.dot_general(
        left, split_right[...], (((0,), (0,)), ((), ())), preferred_element_type=jnp.float32
    )
    out_ref[...] = fisher_ref[...] + product * (1.0 / examples)


def add_product(fisher, left, right, examples):
    t_row, t_col = fisher.shape
    tile = min(512, t_row)
    depth = left.shape[0]
    return pl.pallas_call(
        functools.partial(add_kernel, examples),
        grid=(t_row // tile,),
        out_shape=jax.ShapeDtypeStruct(fisher.shape, fisher.dtype),
        in_specs=[
            pl.BlockSpec((tile, t_col), lambda i: (i, 0)),
            pl.BlockSpec((depth, tile), lambda i: (0, i)),
            pl.BlockSpec((depth, t_col), lambda i: (0, 0)),
        ],
        out_specs=pl.BlockSpec((tile, t_col), lambda i: (i, 0)),
        scratch_shapes=[pltpu.VMEM((3 * depth, t_col), jnp.bfloat16)],
        compiler_params=pltpu.CompilerParams(vmem_limit_bytes=56 * 2**20),
        cost_estimate=pl.CostEstimate(
            flops=6 * depth * t_row * t_col, bytes_accessed=8 * t_row * t_col, transcendentals=0
        ),
        name="add_product",
    )(fisher, left, right)


def body(fisher, slab):
    n_row = lax.axis_size("row")
    n_col = lax.axis_size("col")
    rows, order = slab.shape
    t_row = order // n_row
    t_col = order // n_col
    examples = rows * n_row * n_col
    left, right = gather(slab, n_row, n_col, t_row, t_col)
    return add_product(fisher, left.reshape(examples, t_row), right.reshape(examples, t_col), examples)


def solution(mesh):
    return jax.shard_map(
        body,
        mesh=mesh,
        in_specs=(P("row", "col"), P(("row", "col"), None)),
        out_specs=P("row", "col"),
        check_vma=False,
    )
```

time: 171 us -> 115 us (0.67)
  Pallas kernels: 0 us -> 114 us
  waiting for transfers between devices: 65.1 us -> 0 us
  blocking collectives: 45.6 us -> 0 us
  matrix products: 39.5 us -> 0 us
  between operations: 13.4 us -> 0.01 us
  local copies, waits for them, and re-layouts: 6.59 us -> 0 us
    pallas_call x0 -> x2, Pallas kernels: none -> 114 us  [the longest x1 84.2 us: gather(): pl.pallas_call(functools.partial(gather_kernel, n_row, n_col), out_shape=...]
    all_gather x2 -> x0, waiting for transfers between devices: 65 us -> none  [the longest x1 49.2 us: row_panel(): lax.all_gather(pieces.reshape(rows, n_row, 1, t_row), 'col', axis=2, tile...]
    all_to_all x2 -> x0, blocking collectives: 45.6 us -> none  [the longest x1 32 us: col_pieces(): lax.all_to_all(slab.reshape(rows, n_col, t_col), 'col', split_axis=1, con...]
    dot_general x1 -> x0, matrix products: 39.5 us -> none  [transposed_product(): lax.dot_general(left, right, (((0, 1, 2), (0, 1, 2)), ((), ())), precisio...]
    dot_general x1 -> x0, local copies, waits for them, and re-layouts: 6.59 us -> none  [transposed_product(): lax.dot_general(left, right, (((0, 1, 2), (0, 1, 2)), ((), ())), precisio...]
  transfers between devices with their start and end apart: 2 -> 0, of which waited for: 2 -> 0; matrix products, arithmetic and copies ran while one was open for 4% -> 0% of each run, Pallas kernels for 0% -> 0%
where the time goes in v1:
time: 115 us; the launch traced here: 114 us
  Pallas kernels  114 us (99%)
    pallas_call x1, Pallas kernels, gather(): pl.pallas_call(functools.partial(gather_kernel, n_row, n_col), out_shape=...  84.2 us
    pallas_call x1, Pallas kernels, add_product(): pl.pallas_call(functools.partial(add_kernel, examples), grid=(t_row // ti...  30.2 us

profile of v1, /device:TPU:0, one launch (start us, length us, event | category | flops | bytes accessed | tf_op | source)
XLA Modules:
  0.0 114.4 jit_solution(16751015395646670282)
XLA Ops:
  0.0 84.2 %gather_panels.1 = (f32[8,4,8,4096]{3,2,1,0:T(8,128)}, f32[8,4,8,2048]{3,2,1,0:T(8,128)}) custom-call(f32[8,16384]{1,0:T(8,128)} %slab_ref.1), custom_call_target="tpu_custom_call" | custom-call | tf_op jit(solution)/shard_map/gather_panels/pallas_call | solution.py:253
  84.2 30.2 %add_product.1 = f32[4096,2048]{1,0:T(8,128)} custom-call(f32[4096,2048]{1,0:T(8,128)} %fisher_ref.1, f32[256,4096]{1,0:T(8,128)} %bitcast.2, f32[256,2048]{1,0:T(8,128)} %bitcast.3), custom_call_target="tpu_custom_call" | custom-call | flops 12884901888 | bytes 67108864 | tf_op jit(solution)/shard_map/add_product/pallas_call | solution.py:298
